TPU v7x, 256 devices: a whole 4x4x8 slice. The times are simulated.
256 devices in a mesh: frame: 128 (over z, x, y), track: 2 (over core).
Axes of the slice: x: 4, y: 4, z: 8, core: 2. Of those that a mesh axis runs over, the one named last changes fastest.
Arguments:
- feature_maps: bfloat16 [256, 4096, 256], P('frame'), may hold values from -16 to 16
- query_frame: int32 [1024], P('track'), may hold values from 0 to 255
- query_pixel: int32 [2, 1024], P(None, 'track'), may hold values from 0 to 63
- conv_kernel: float32 [3, 512], replicated, may hold values from -3 to 3
- norm_gain: float32 [512], replicated, may hold values from 0.5 to 1.5
- w_in: bfloat16 [2048, 512], P('track'), may hold values from -0.25 to 0.25
- w_out: bfloat16 [2048, 256], P('track'), may hold values from -0.125 to 0.125
Outputs:
- coarse_points: float32 [2, 256, 1024], P(None, 'frame', 'track')
- refined_points: float32 [2, 256, 1024], P(None, 'frame', 'track')
All inputs are finite; a program needn't handle non-finite values.
Results may differ from a plain program's by a relative error of at most 0.0035.
The roundings to bfloat16 on the way count: a program that leaves them out, or rounds other values in their place, can miss the bound.
Values may be sent and summed in bfloat16 or wider, within the bound.
A program may use at most 128 MiB of HBM per device.

v0:
```python
import jax
import jax.numpy as jnp
from jax import lax
from jax.sharding import Mesh
from jax.sharding import PartitionSpec as P

C = 256
SIDE = 64
KT = 3
FRAME = ("z", "x", "y")


def soft_argmax(queries, frame_map):
    scores = jnp.einsum(
        "tc,pc->tp", queries, frame_map, preferred_element_type=jnp.float32
    ) * C ** (-0.5)
    peak = jnp.max(scores, axis=1, keepdims=True)
    expo = jnp.exp(scores - peak)
    weights = expo / jnp.sum(expo, axis=1, keepdims=True)
    centers = (jnp.arange(SIDE, dtype=jnp.float32) + 0.5) * (2.0 / SIDE) - 1.0
    rows = jnp.repeat(centers, SIDE)
    columns = jnp.tile(centers, SIDE)
    vertical = jnp.sum(weights * rows, axis=1)
    horizontal = jnp.sum(weights * columns, axis=1)
    return (weights, vertical, horizontal)


def local(feature_maps, query_frame, query_pixel, conv_kernel, norm_gain, w_in, w_out):
    frames_here = feature_maps.shape[0]
    index = lax.axis_index(FRAME)
    count = lax.axis_size(FRAME)
    w_in = lax.all_gather(w_in, "track", axis=0, tiled=True)
    w_out = lax.all_gather(w_out, "track", axis=0, tiled=True)
    flat_maps = feature_maps.reshape(-1, C)
    offset_frame = query_frame - index * frames_here
    owned = (offset_frame >= 0) & (offset_frame < frames_here)
    flat_rows = (
        jnp.clip(offset_frame, 0, frames_here - 1) * (SIDE * SIDE)
        + query_pixel[0] * SIDE
        + query_pixel[1]
    )
    queries = jnp.where(owned[:, None], flat_maps[flat_rows], 0)
    for axis in ("z", "x", "y"):
        queries = lax.psum(queries, axis)
    sampled_list = []
    coarse = []
    for slot in range(frames_here):
        weights, vertical, horizontal = soft_argmax(queries, feature_maps[slot])
        sampled_list.append(
            jnp.dot(
                weights.astype(jnp.bfloat16), feature_maps[slot], preferred_element_type=jnp.float32
            ).astype(jnp.bfloat16)
        )
        coarse.append(jnp.stack([vertical, horizontal], 0))
    from_left = lax.ppermute(sampled_list[-1], FRAME, [(i, i + 1) for i in range(count - 1)])
    from_right = lax.ppermute(sampled_list[0], FRAME, [(i + 1, i) for i in range(count - 1)])
    window = [from_left] + sampled_list + [from_right]
    inside = [(index > 0).astype(jnp.float32)] + [1.0] * frames_here
    inside += [(index < count - 1).astype(jnp.float32)]
    refined = []
    for slot in range(frames_here):
        read_part = 0.0
        query_part = 0.0
        for tap in range(KT):
            read_part = read_part + conv_kernel[tap, :C] * window[slot + tap].astype(jnp.float32)
            query_part = query_part + conv_kernel[tap, C:] * inside[slot + tap]
        query_part = query_part * queries.astype(jnp.float32)
        blended = jnp.concatenate([read_part, query_part], axis=-1)
        normed = (
            blended
            * lax.rsqrt(jnp.mean(blended * blended, axis=1, keepdims=True) + 1e-06)
            * norm_gain
        ).astype(jnp.bfloat16)
        hidden = jnp.einsum("rm,hm->rh", normed, w_in, preferred_element_type=jnp.float32)
        hidden = jax.nn.gelu(hidden).astype(jnp.bfloat16)
        update = jnp.dot(hidden, w_out, preferred_element_type=jnp.float32)
        updated = (blended[:, :C] + update).astype(jnp.bfloat16)
        _, vertical, horizontal = soft_argmax(updated, feature_maps[slot])
        refined.append(jnp.stack([vertical, horizontal], 0))
    return (jnp.stack(coarse, 1), jnp.stack(refined, 1))


def solution(mesh):
    sizes = {"y": 4, "x": 4}
    z = mesh.shape["frame"] // 16
    split = Mesh(
        mesh.devices.reshape(z, sizes["x"], sizes["y"], mesh.shape["track"]),
        ("z", "x", "y", "track"),
    )
    in_specs = (
        P(FRAME, None, None),
        P("track"),
        P(None, "track"),
        P(),
        P(),
        P("track", None),
        P("track", None),
    )
    out_specs = (P(None, FRAME, "track"), P(None, FRAME, "track"))
    return jax.shard_map(local, mesh=split, in_specs=in_specs, out_specs=out_specs, check_vma=False)
```

profile of v0, /device:TPU:126, one launch (start us, length us, event | category | flops | bytes accessed | tf_op | source)
XLA Modules:
  0.0 278.4 jit_solution(8686620003232133565)
XLA Ops:
  8.0 0.8 slice_multiply_fusion
  8.8 0.7 compare_and_fusion
  9.5 0.7 compare_select_fusion
  10.2 4.3 %gather_fusion = bf16[512,256]{1,0:T(8,128)(2,1)S(1)} fusion(bf16[8192,256]{1,0:T(8,128)(2,1)} %bitcast.56, s32[1024]{0:T(1024)S(1)} %pad_clamp_fusion), kind=kCustom, calls=%fused_computation | custom fusion | bytes 526336 | tf_op jit(solution)/shard_map/gather | solution.py:42
  14.6 0.7 broadcast_select_fusion
  15.4 73.4 %all-reduce.4.cloned.1.call-done = bf16[512,256]{0,1:T(8,128)(2,1)} async-done(((bf16[512,256]{0,1:T(8,128)(2,1)}), bf16[512,256]{0,1:T(8,128)(2,1)}) %all-reduce.4.cloned.1.call-update) | async-done | bytes 262160 | tf_op jit(solution)/shard_map/psum | solution.py:44
  89.0 47.2 %all-reduce.6.cloned.1.call-done = bf16[512,256]{0,1:T(8,128)(2,1)} async-done(((bf16[512,256]{0,1:T(8,128)(2,1)}), bf16[512,256]{0,1:T(8,128)(2,1)}) %all-reduce.6.cloned.1.call-update) | async-done | bytes 262160 | tf_op jit(solution)/shard_map/psum | solution.py:44
  136.3 0.5 all-gather.3.cloned.1.call-update
  136.8 0.5 all-gather.5.cloned.1.call-update
  137.4 0.8 multiply_add_fusion
  138.2 47.6 %all-reduce.8.cloned.1.call-done = bf16[512,256]{0,1:T(8,128)(2,1)} async-done(((bf16[512,256]{0,1:T(8,128)(2,1)}), bf16[512,256]{0,1:T(8,128)(2,1)}) %all-reduce.8.cloned.1.call-update) | async-done | bytes 262160 | tf_op jit(solution)/shard_map/psum | solution.py:44
  185.8 3.2 %multiply_reduce_fusion.10 = (f32[512]{0:T(512)S(1)}, f32[512,4096]{1,0:T(8,128)S(1)}) fusion(bf16[512,256]{0,1:T(8,128)(2,1)} %all-reduce.8.cloned.1.call-done, bf16[2,4096,256]{2,1,0:T(8,128)(2,1)} %param.7), kind=kOutput, calls=%fused_computation.15 | convolution fusion | flops 1077935616 | bytes 10749952 | tf_op jit(solution)/shard_map/tc,pc->tp/dot_general | solution.py:14
  189.0 1.5 fusion.3
  190.6 2.2 fusion.54
  192.8 5.9 %collective-permute-start = (bf16[512,256]{0,1:T(8,128)(2,1)S(1)}, bf16[512,256]{0,1:T(8,128)(2,1)S(1)}, u32[]{:S(2)}, u32[]{:S(2)}) collective-permute-start(bf16[512,256]{0,1:T(8,128)(2,1)S(1)} %fusion.54), channel_id=1, source_target_pairs={{0,2},{2,4},{4,6},{6,8},{8,10},{10,12},{12,14},{14,16},{16,18},{18... | collective-permute-start | bytes 786440 | tf_op jit(solution)/shard_map/ppermute | solution.py:55
  198.7 1.4 multiply_reduce_fusion.11
  200.1 1.5 fusion.1
  201.6 2.2 fusion.59
  203.8 2.1 collective-permute-start.1
  206.4 11.1 %collective-permute-done.1 = bf16[512,256]{0,1:T(8,128)(2,1)S(1)} collective-permute-done((bf16[512,256]{0,1:T(8,128)(2,1)S(1)}, bf16[512,256]{0,1:T(8,128)(2,1)S(1)}, u32[]{:S(2)}, u32[]{:S(2)}) %collective-permute-start.1) | collective-permute-done | bytes 262176 | tf_op jit(solution)/shard_map/ppermute | solution.py:56
  217.5 0.3 fusion.77
  217.8 0.2 multiply_reduce_fusion.12
  218.1 5.0 %fusion.79 = f32[512,2048]{1,0:T(8,128)} fusion(bf16[2048,512]{1,0:T(8,128)(2,1)} %all-gather.3.cloned.1.call-done, f32[512,256]{0,1:T(8,128)S(1)} %get-tuple-element.20, f32[512,256]{0,1:T(8,128)S(1)} %get-tuple-element.18, f32[512]{0:T(512)S(1)} %add_rsqrt_fusion, f32[512]{0:T(512)S(1)} %copy-done.6), kind=kOutput, calls=%fused_computation.88 | convolution fusion | flops 1074790400 | bytes 7344128 | tf_op jit(solution)/shard_map/rm,hm->rh/dot_general | solution.py:74
  223.2 9.4 %multiply_reduce_fusion.8 = (f32[512]{0:T(512)S(1)}, f32[512,4096]{1,0:T(8,128)}) fusion(bf16[2,4096,256]{2,1,0:T(8,128)(2,1)} %param.7, f32[512,256]{0,1:T(8,128)S(1)} %get-tuple-element.18, bf16[2048,256]{1,0:T(8,128)(2,1)} %all-gather.5.cloned.1.call-done, f32[512,2048]{1,0:T(8,128)} %fusion.79), kind=kOutput, calls=%fused_computation.13 | convolution fusion | flops 1624505856 | bytes 16254976 | tf_op jit(solution)/shard_map/tc,pc->tp/dot_general | solution.py:14
  232.5 5.0 %fusion.7 = f32[512]{0:T(512)S(1)} fusion(f32[512,4096]{1,0:T(8,128)} %get-tuple-element.36, f32[512]{0:T(512)S(1)} %get-tuple-element.35), kind=kLoop, calls=%fused_computation.24 | loop fusion | flops 6290944 | bytes 8392704 | tf_op jit(solution)/shard_map/reduce_sum | solution.py:19
  237.6 3.5 %fusion.78 = f32[512,2048]{1,0:T(8,128)} fusion(bf16[2048,512]{1,0:T(8,128)(2,1)S(1)} %copy-done.4, f32[512,256]{0,1:T(8,128)S(1)} %get-tuple-element.21, f32[512,256]{0,1:T(8,128)S(1)} %get-tuple-element.19, f32[512]{0:T(512)S(1)} %copy-done.6, f32[512]{0:T(512)S(1)} %add_rsqrt_fusion.1), kind=kOutput, calls=%fused_computation.87 | convolution fusion | flops 1074790400 | bytes 7344128 | tf_op jit(solution)/shard_map/rm,hm->rh/dot_general | solution.py:74
  241.1 9.3 %multiply_reduce_fusion.9 = (f32[512]{0:T(512)S(1)}, f32[512,4096]{1,0:T(8,128)}) fusion(bf16[2,4096,256]{2,1,0:T(8,128)(2,1)} %param.7, f32[512,256]{0,1:T(8,128)S(1)} %get-tuple-element.19, bf16[2048,256]{1,0:T(8,128)(2,1)} %all-gather.5.cloned.1.call-done, f32[512,2048]{1,0:T(8,128)} %fusion.78), kind=kOutput, calls=%fused_computation.14 | convolution fusion | flops 1624505856 | bytes 16254976 | tf_op jit(solution)/shard_map/tc,pc->tp/dot_general | solution.py:14
  250.4 5.3 %fusion.5 = f32[512]{0:T(512)S(1)} fusion(f32[512,4096]{1,0:T(8,128)} %get-tuple-element.34, f32[512]{0:T(512)S(1)} %get-tuple-element.33), kind=kLoop, calls=%fused_computation.22 | loop fusion | flops 6290944 | bytes 8392704 | tf_op jit(solution)/shard_map/reduce_sum | solution.py:19
  255.7 0.5 copy-done.2
  256.2 13.8 %multiply_reduce_fusion.5 = (f32[512]{0:T(512)S(1)}, f32[512]{0:T(512)S(1)}, f32[512]{0:T(512)S(1)}, f32[512]{0:T(512)S(1)}, f32[512]{0:T(512)S(1)}, /*index=5*/f32[512]{0:T(512)S(1)}, f32[512]{0:T(512)S(1)}, f32[512]{0:T(512)S(1)}) fusion(f32[4096]{0:T(1024)S(1)} %mul.292, f32[4096]{0:T(1024)S(1)} %mul.295, f32[512]{0:T(512)S(1)} %fusion.5, ...), kind=kLoop, calls=%fused_computation.8 | loop fusion | flops 58716160 | bytes 33619968 | tf_op jit(solution)/shard_map/reduce_sum | solution.py:23
  270.1 0.6 copy.12
  270.7 0.6 copy.11
  (40 shorter events, 0.9 us)
Async XLA Ops:
  8.0 80.9 %all-reduce.4.cloned.1.call-start = ((), (), s32[]{:S(2)}) async-start(), calls=%async_computation | async-start | bytes 524288 | tf_op jit(solution)/shard_map/psum | solution.py:44
  15.4 120.8 %all-reduce.6.cloned.1.call-start = ((), (), s32[]{:S(2)}) async-start(), calls=%async_computation.1 | async-start | bytes 524288 | tf_op jit(solution)/shard_map/psum | solution.py:44
  88.9 96.9 %all-reduce.8.cloned.1.call-start = ((), (), s32[]{:S(2)}) async-start(), calls=%async_computation.2 | async-start | bytes 524288 | tf_op jit(solution)/shard_map/psum | solution.py:44
  136.2 81.9 %all-gather.3.cloned.1.call-start = ((), (), s32[]{:S(2)}) async-start(), calls=%async_computation.3 | async-start | bytes 3145728 | tf_op jit(solution)/shard_map/all_gather | solution.py:32
  136.8 86.4 %all-gather.5.cloned.1.call-start = ((), (), s32[]{:S(2)}) async-start(), calls=%async_computation.4 | async-start | bytes 1572864 | tf_op jit(solution)/shard_map/all_gather | solution.py:33
  185.8 4.7 %copy-start.3 = (bf16[2,4096,256]{2,1,0:T(8,128)(2,1)S(1)}, bf16[2,4096,256]{2,1,0:T(8,128)(2,1)}, u32[]{:S(2)}) copy-start(bf16[2,4096,256]{2,1,0:T(8,128)(2,1)} %param.7) | copy-start | bytes 12582916
  189.0 3.7 %copy-start = (f32[512,4096]{1,0:T(8,128)}, f32[512,4096]{1,0:T(8,128)S(1)}, u32[]{:S(2)}) copy-start(f32[512,4096]{1,0:T(8,128)S(1)} %get-tuple-element.30) | copy-start | bytes 25165828
  190.5 8.1 %copy-start.5 = (bf16[512,256]{0,1:T(8,128)(2,1)S(1)}, bf16[512,256]{0,1:T(8,128)(2,1)}, u32[]{:S(2)}) copy-start(bf16[512,256]{0,1:T(8,128)(2,1)} %all-reduce.8.cloned.1.call-done) | copy-start | bytes 786436
  192.8 13.6 %collective-permute-start = (bf16[512,256]{0,1:T(8,128)(2,1)S(1)}, bf16[512,256]{0,1:T(8,128)(2,1)S(1)}, u32[]{:S(2)}, u32[]{:S(2)}) collective-permute-start(bf16[512,256]{0,1:T(8,128)(2,1)S(1)} %fusion.54), channel_id=1, source_target_pairs={{0,2},{2,4},{4,6},{6,8},{8,10},{10,12},{12,14},{14,16},{16,18},{18... | collective-permute-start | bytes 786440 | tf_op jit(solution)/shard_map/ppermute | solution.py:55
  200.1 3.7 %copy-start.1 = (f32[512,4096]{1,0:T(8,128)}, f32[512,4096]{1,0:T(8,128)S(1)}, u32[]{:S(2)}) copy-start(f32[512,4096]{1,0:T(8,128)S(1)} %get-tuple-element.32) | copy-start | bytes 25165828
  201.6 16.5 %copy-start.6 = (f32[512]{0:T(512)S(1)}, f32[512]{0:T(512)}, u32[]{:S(2)}) copy-start(f32[512]{0:T(512)} %param.11) | copy-start | bytes 6148
  203.8 13.7 %collective-permute-start.1 = (bf16[512,256]{0,1:T(8,128)(2,1)S(1)}, bf16[512,256]{0,1:T(8,128)(2,1)S(1)}, u32[]{:S(2)}, u32[]{:S(2)}) collective-permute-start(bf16[512,256]{0,1:T(8,128)(2,1)S(1)} %fusion.59), channel_id=1, source_target_pairs={{2,0},{4,2},{6,4},{8,6},{10,8},{12,10},{14,12},{16,14},{18,16},{20... | collective-permute-start | bytes 786440 | tf_op jit(solution)/shard_map/ppermute | solution.py:56
  232.5 5.0 %copy-start.4 = (bf16[2048,512]{1,0:T(8,128)(2,1)S(1)}, bf16[2048,512]{1,0:T(8,128)(2,1)}, u32[]{:S(2)}) copy-start(bf16[2048,512]{1,0:T(8,128)(2,1)} %all-gather.3.cloned.1.call-done) | copy-start | bytes 6291460
  250.4 5.8 %copy-start.2 = (f32[512,4096]{1,0:T(8,128)S(1)}, f32[512,4096]{1,0:T(8,128)}, u32[]{:S(2)}) copy-start(f32[512,4096]{1,0:T(8,128)} %get-tuple-element.34) | copy-start | bytes 25165828
Sparse Core Ops, SparseCore 0:
  15.5 73.3 all-reduce.3
  91.3 44.8 all-reduce.5
  138.5 47.2 all-reduce.7
Sparse Core Ops, SparseCore 1:
  138.6 17.4 all-gather.2
  157.9 15.5 all-gather.4
where the time goes:
time: 279 us; the launch traced here: 278 us
  waiting for transfers between devices  181 us (65%)
  matrix products  36.3 us (13%)
  other arithmetic  31.5 us (11%)
  between operations  15.4 us (6%)
  starting transfers between devices  8.24 us (3%)
  local copies, waits for them, and re-layouts  6.37 us (2%)
    psum x3, waiting for transfers between devices, local(): queries = lax.psum(queries, axis)  168 us
    dot_general x4, matrix products, soft_argmax(): jnp.einsum('tc,pc->tp', queries, frame_map, preferred_element_type=jnp.fl...  23.3 us
    reduce_sum x1, other arithmetic, soft_argmax(): vertical = jnp.sum(weights * rows, axis=1)  13.8 us
    reduce_sum x4, other arithmetic, soft_argmax(): weights = expo / jnp.sum(expo, axis=1, keepdims=True)  13.3 us
    ppermute x1, waiting for transfers between devices, local(): lax.ppermute(sampled_list[0], FRAME, [(i + 1, i) for i in range(count - 1)])  11.1 us
    dot_general x2, matrix products, local(): jnp.einsum('rm,hm->rh', normed, w_in, preferred_element_type=jnp.float32)  8.57 us
    ppermute x1, starting transfers between devices, local(): lax.ppermute(sampled_list[-1], FRAME, [(i, i + 1) for i in range(count -...  5.9 us
  transfers between devices with their start and end apart: 7, of which 4 were waited for; matrix products, arithmetic and copies ran while one was open for 7% of the time, Pallas kernels for 0%

commit v1 on v0

--- a/solution.py
+++ b/solution.py
@@ -41,7 +41,7 @@
     )
     queries = jnp.where(owned[:, None], flat_maps[flat_rows], 0)
     for axis in ("z", "x", "y"):
-        queries = lax.psum(queries, axis)
+        queries = jnp.sum(lax.all_gather(queries, axis), axis=0)
     sampled_list = []
     coarse = []
     for slot in range(frames_here):

time: 279 us -> 208 us (0.75)
  waiting for transfers between devices: 181 us -> 106 us
  other arithmetic: 31.5 us -> 37.1 us
    psum x3 -> x0, waiting for transfers between devices: 168 us -> none  [local(): queries = lax.psum(queries, axis)]
    all_gather x0 -> x3, waiting for transfers between devices: none -> 92.8 us  [local(): queries = jnp.sum(lax.all_gather(queries, axis), axis=0)]
    reduce_sum x0 -> x3, other arithmetic: none -> 6.29 us  [local(): queries = jnp.sum(lax.all_gather(queries, axis), axis=0)]
  transfers between devices with their start and end apart: 7 -> 7, of which waited for: 4 -> 4; matrix products, arithmetic and copies ran while one was open for 7% -> 9% of each run, Pallas kernels for 0% -> 0%
where the time goes in v1:
time: 208 us
  waiting for transfers between devices  106 us (51%)
  other arithmetic  37.1 us (18%)
  matrix products  36.3 us (17%)
  between operations  14 us (7%)
  starting transfers between devices  7.87 us (4%)
  local copies, waits for them, and re-layouts  6.75 us (3%)
    all_gather x3, waiting for transfers between devices, local(): queries = jnp.sum(lax.all_gather(queries, axis), axis=0)  92.8 us
    dot_general x4, matrix products, soft_argmax(): jnp.einsum('tc,pc->tp', queries, frame_map, preferred_element_type=jnp.fl...  23.2 us
    reduce_sum x1, other arithmetic, soft_argmax(): vertical = jnp.sum(weights * rows, axis=1)  13.8 us
    reduce_sum x4, other arithmetic, soft_argmax(): weights = expo / jnp.sum(expo, axis=1, keepdims=True)  13.3 us
    ppermute x1, waiting for transfers between devices, local(): lax.ppermute(sampled_list[0], FRAME, [(i + 1, i) for i in range(count - 1)])  11.7 us
    dot_general x2, matrix products, local(): jnp.einsum('rm,hm->rh', normed, w_in, preferred_element_type=jnp.float32)  8.72 us
    reduce_sum x3, other arithmetic, local(): queries = jnp.sum(lax.all_gather(queries, axis), axis=0)  6.29 us
    ppermute x1, starting transfers between devices, local(): lax.ppermute(sampled_list[-1], FRAME, [(i, i + 1) for i in range(count -...  5.75 us
  transfers between devices with their start and end apart: 7, of which 4 were waited for; matrix products, arithmetic and copies ran while one was open for 9% of the time, Pallas kernels for 0%

profile of v1, /device:TPU:126, one launch (start us, length us, event | category | flops | bytes accessed | tf_op | source)
XLA Modules:
  0.0 207.7 jit_solution(1336732956706749837)
XLA Ops:
  7.2 0.8 slice_multiply_fusion
  8.0 0.7 compare_and_fusion
  8.7 0.7 compare_select_fusion
  9.4 4.3 %gather_fusion = bf16[512,256]{1,0:T(8,128)(2,1)S(1)} fusion(bf16[8192,256]{1,0:T(8,128)(2,1)} %bitcast.60, s32[1024]{0:T(1024)S(1)} %pad_clamp_fusion), kind=kCustom, calls=%fused_computation | custom fusion | bytes 526336 | tf_op jit(solution)/shard_map/gather | solution.py:42
  13.7 0.9 bitcast_select_fusion
  14.6 41.9 %all-gather.8.cloned.1.call-done = bf16[8,512,256]{2,1,0:T(8,128)(2,1)} async-done(((bf16[1,512,256]{2,1,0:T(8,128)(2,1)}), bf16[8,512,256]{2,1,0:T(8,128)(2,1)}) %all-gather.8.cloned.1.call-update) | async-done | bytes 2097168 | tf_op jit(solution)/shard_map/all_gather | solution.py:44
  56.6 2.7 %reduce_sum.162 = bf16[512,256]{1,0:T(8,128)(2,1)} reduce(bf16[8,512,256]{2,1,0:T(8,128)(2,1)} %all-gather.8.cloned.1.call-done, bf16[]{:T(256)} %constant.23.clone.1), dimensions={0}, to_apply=%region_0.1 | reduce | flops 917504 | bytes 2359298 | tf_op jit(solution)/shard_map/reduce_sum | solution.py:44
  59.3 25.1 %all-gather.14.cloned.1.call-done = bf16[2048,256]{1,0:T(8,128)(2,1)} async-done(((bf16[512,256]{1,0:T(8,128)(2,1)}), bf16[2048,256]{1,0:T(8,128)(2,1)}) %all-gather.14.cloned.1.call-update) | async-done | bytes 1048592 | tf_op jit(solution)/shard_map/all_gather | solution.py:44
  84.4 2.2 %reduce_sum.163 = bf16[512,256]{1,0:T(8,128)(2,1)} reduce(bf16[4,512,256]{2,1,0:T(8,128)(2,1)} %bitcast.62, bf16[]{:T(256)} %constant.23.clone.1), dimensions={0}, to_apply=%region_1.2 | reduce | flops 393216 | bytes 1310722 | tf_op jit(solution)/shard_map/reduce_sum | solution.py:44
  86.6 0.5 all-gather.10.cloned.1.call-update
  87.2 0.5 all-gather.12.cloned.1.call-update
  87.7 25.8 %all-gather.16.cloned.1.call-done = bf16[2048,256]{1,0:T(8,128)(2,1)} async-done(((bf16[512,256]{1,0:T(8,128)(2,1)}), bf16[2048,256]{1,0:T(8,128)(2,1)}) %all-gather.16.cloned.1.call-update) | async-done | bytes 1048592 | tf_op jit(solution)/shard_map/all_gather | solution.py:44
  113.5 1.5 reduce_sum.164
  115.0 3.1 %multiply_reduce_fusion.10 = (f32[512]{0:T(512)S(1)}, f32[512,4096]{1,0:T(8,128)S(1)}) fusion(bf16[512,256]{1,0:T(8,128)(2,1)S(1)} %reduce_sum.164, bf16[2,4096,256]{2,1,0:T(8,128)(2,1)} %param.7), kind=kOutput, calls=%fused_computation.15 | convolution fusion | flops 1077935616 | bytes 10749952 | tf_op jit(solution)/shard_map/tc,pc->tp/dot_general | solution.py:14
  118.1 1.4 multiply_reduce_fusion.11
  119.5 1.5 fusion.3
  121.4 2.2 %fusion.54 = bf16[512,256]{0,1:T(8,128)(2,1)S(1)} fusion(bf16[2,4096,256]{2,1,0:T(8,128)(2,1)S(1)} %copy-done.3, f32[512,4096]{1,0:T(8,128)S(1)} %get-tuple-element.34, f32[512]{0:T(512)S(1)} %fusion.3, f32[512]{0:T(512)S(1)} %get-tuple-element.33), kind=kOutput, calls=%fused_computation.67 | convolution fusion | flops 1082261504 | bytes 10752000 | tf_op jit(solution)/shard_map/dot_general | solution.py:50
  123.6 5.8 %collective-permute-start = (bf16[512,256]{0,1:T(8,128)(2,1)S(1)}, bf16[512,256]{0,1:T(8,128)(2,1)S(1)}, u32[]{:S(2)}, u32[]{:S(2)}) collective-permute-start(bf16[512,256]{0,1:T(8,128)(2,1)S(1)} %fusion.54), channel_id=1, source_target_pairs={{0,2},{2,4},{4,6},{6,8},{8,10},{10,12},{12,14},{14,16},{16,18},{18... | collective-permute-start | bytes 786440 | tf_op jit(solution)/shard_map/ppermute | solution.py:55
  129.3 1.5 fusion.1
  130.8 2.2 %fusion.59 = bf16[512,256]{0,1:T(8,128)(2,1)S(1)} fusion(bf16[2,4096,256]{2,1,0:T(8,128)(2,1)S(1)} %copy-done.3, f32[512,4096]{1,0:T(8,128)S(1)} %get-tuple-element.36, f32[512]{0:T(512)S(1)} %fusion.1, f32[512]{0:T(512)S(1)} %get-tuple-element.35), kind=kOutput, calls=%fused_computation.68 | convolution fusion | flops 1082261504 | bytes 10752000 | tf_op jit(solution)/shard_map/dot_general | solution.py:50
  133.1 1.9 collective-permute-start.1
  135.5 11.7 %collective-permute-done.1 = bf16[512,256]{0,1:T(8,128)(2,1)S(1)} collective-permute-done((bf16[512,256]{0,1:T(8,128)(2,1)S(1)}, bf16[512,256]{0,1:T(8,128)(2,1)S(1)}, u32[]{:S(2)}, u32[]{:S(2)}) %collective-permute-start.1) | collective-permute-done | bytes 262176 | tf_op jit(solution)/shard_map/ppermute | solution.py:56
  147.8 5.2 %fusion.79 = f32[512,2048]{1,0:T(8,128)} fusion(bf16[2048,512]{1,0:T(8,128)(2,1)} %all-gather.10.cloned.1.call-done, f32[512,256]{0,1:T(8,128)S(1)} %get-tuple-element.24, f32[512,256]{0,1:T(8,128)S(1)} %get-tuple-element.22, f32[512]{0:T(512)S(1)} %add_rsqrt_fusion, f32[512]{0:T(512)S(1)} %copy-done.5), kind=kOutput, calls=%fused_computation.88 | convolution fusion | flops 1074790400 | bytes 7344128 | tf_op jit(solution)/shard_map/rm,hm->rh/dot_general | solution.py:74
  153.0 9.4 %multiply_reduce_fusion.8 = (f32[512]{0:T(512)S(1)}, f32[512,4096]{1,0:T(8,128)}) fusion(bf16[2,4096,256]{2,1,0:T(8,128)(2,1)} %param.7, f32[512,256]{0,1:T(8,128)S(1)} %get-tuple-element.22, bf16[2048,256]{1,0:T(8,128)(2,1)} %all-gather.12.cloned.1.call-done, f32[512,2048]{1,0:T(8,128)} %fusion.79), kind=kOutput, calls=%fused_computation.13 | convolution fusion | flops 1624505856 | bytes 16254976 | tf_op jit(solution)/shard_map/tc,pc->tp/dot_general | solution.py:14
  162.4 5.0 %fusion.7 = f32[512]{0:T(512)S(1)} fusion(f32[512,4096]{1,0:T(8,128)} %get-tuple-element.40, f32[512]{0:T(512)S(1)} %get-tuple-element.39), kind=kLoop, calls=%fused_computation.24 | loop fusion | flops 6290944 | bytes 8392704 | tf_op jit(solution)/shard_map/reduce_sum | solution.py:19
  167.4 3.5 %fusion.78 = f32[512,2048]{1,0:T(8,128)} fusion(bf16[2048,512]{1,0:T(8,128)(2,1)S(1)} %copy-done.4, f32[512,256]{0,1:T(8,128)S(1)} %get-tuple-element.25, f32[512,256]{0,1:T(8,128)S(1)} %get-tuple-element.23, f32[512]{0:T(512)S(1)} %copy-done.5, f32[512]{0:T(512)S(1)} %add_rsqrt_fusion.1), kind=kOutput, calls=%fused_computation.87 | convolution fusion | flops 1074790400 | bytes 7344128 | tf_op jit(solution)/shard_map/rm,hm->rh/dot_general | solution.py:74
  171.0 9.3 %multiply_reduce_fusion.9 = (f32[512]{0:T(512)S(1)}, f32[512,4096]{1,0:T(8,128)}) fusion(bf16[2,4096,256]{2,1,0:T(8,128)(2,1)} %param.7, f32[512,256]{0,1:T(8,128)S(1)} %get-tuple-element.23, bf16[2048,256]{1,0:T(8,128)(2,1)} %all-gather.12.cloned.1.call-done, f32[512,2048]{1,0:T(8,128)} %fusion.78), kind=kOutput, calls=%fused_computation.14 | convolution fusion | flops 1624505856 | bytes 16254976 | tf_op jit(solution)/shard_map/tc,pc->tp/dot_general | solution.py:14
  180.3 5.2 %fusion.5 = f32[512]{0:T(512)S(1)} fusion(f32[512,4096]{1,0:T(8,128)} %get-tuple-element.38, f32[512]{0:T(512)S(1)} %get-tuple-element.37), kind=kLoop, calls=%fused_computation.22 | loop fusion | flops 6290944 | bytes 8392704 | tf_op jit(solution)/shard_map/reduce_sum | solution.py:19
  185.5 0.5 copy-done.2
  186.1 13.8 %multiply_reduce_fusion.5 = (f32[512]{0:T(512)S(1)}, f32[512]{0:T(512)S(1)}, f32[512]{0:T(512)S(1)}, f32[512]{0:T(512)S(1)}, f32[512]{0:T(512)S(1)}, /*index=5*/f32[512]{0:T(512)S(1)}, f32[512]{0:T(512)S(1)}, f32[512]{0:T(512)S(1)}) fusion(f32[4096]{0:T(1024)S(1)} %mul.292, f32[4096]{0:T(1024)S(1)} %mul.295, f32[512]{0:T(512)S(1)} %fusion.5, ...), kind=kLoop, calls=%fused_computation.8 | loop fusion | flops 58716160 | bytes 33619968 | tf_op jit(solution)/shard_map/reduce_sum | solution.py:23
  199.9 0.6 copy.19
  200.6 0.6 copy.18
  (43 shorter events, 1.8 us)
Async XLA Ops:
  7.2 80.6 %copy-start.6 = (f32[3,512]{1,0:T(4,128)S(1)}, f32[3,512]{1,0:T(4,128)}, u32[]{:S(2)}) copy-start(f32[3,512]{1,0:T(4,128)} %param.10) | copy-start | bytes 18436
  7.2 49.4 %all-gather.8.cloned.1.call-start = ((), (), s32[]{:S(2)}) async-start(), calls=%async_computation | async-start | bytes 2359296 | tf_op jit(solution)/shard_map/all_gather | solution.py:44
  14.6 69.8 %all-gather.14.cloned.1.call-start = ((), (), s32[]{:S(2)}) async-start(), calls=%async_computation.3 | async-start | bytes 1310720 | tf_op jit(solution)/shard_map/all_gather | solution.py:44
  59.2 54.3 %all-gather.16.cloned.1.call-start = ((), (), s32[]{:S(2)}) async-start(), calls=%async_computation.4 | async-start | bytes 1310720 | tf_op jit(solution)/shard_map/all_gather | solution.py:44
  86.5 61.3 %all-gather.10.cloned.1.call-start = ((), (), s32[]{:S(2)}) async-start(), calls=%async_computation.1 | async-start | bytes 3145728 | tf_op jit(solution)/shard_map/all_gather | solution.py:32
  87.1 65.9 %all-gather.12.cloned.1.call-start = ((), (), s32[]{:S(2)}) async-start(), calls=%async_computation.2 | async-start | bytes 1572864 | tf_op jit(solution)/shard_map/all_gather | solution.py:33
  115.0 3.1 %copy-start.3 = (bf16[2,4096,256]{2,1,0:T(8,128)(2,1)S(1)}, bf16[2,4096,256]{2,1,0:T(8,128)(2,1)}, u32[]{:S(2)}) copy-start(bf16[2,4096,256]{2,1,0:T(8,128)(2,1)} %param.7) | copy-start | bytes 12582916
  118.1 3.2 %copy-start = (f32[512,4096]{1,0:T(8,128)}, f32[512,4096]{1,0:T(8,128)S(1)}, u32[]{:S(2)}) copy-start(f32[512,4096]{1,0:T(8,128)S(1)} %get-tuple-element.34) | copy-start | bytes 25165828
  119.5 11.3 %copy-start.1 = (f32[512,4096]{1,0:T(8,128)}, f32[512,4096]{1,0:T(8,128)S(1)}, u32[]{:S(2)}) copy-start(f32[512,4096]{1,0:T(8,128)S(1)} %get-tuple-element.36) | copy-start | bytes 25165828
  123.6 12.0 %collective-permute-start = (bf16[512,256]{0,1:T(8,128)(2,1)S(1)}, bf16[512,256]{0,1:T(8,128)(2,1)S(1)}, u32[]{:S(2)}, u32[]{:S(2)}) collective-permute-start(bf16[512,256]{0,1:T(8,128)(2,1)S(1)} %fusion.54), channel_id=1, source_target_pairs={{0,2},{2,4},{4,6},{6,8},{8,10},{10,12},{12,14},{14,16},{16,18},{18... | collective-permute-start | bytes 786440 | tf_op jit(solution)/shard_map/ppermute | solution.py:55
  130.8 17.0 %copy-start.5 = (f32[512]{0:T(512)S(1)}, f32[512]{0:T(512)}, u32[]{:S(2)}) copy-start(f32[512]{0:T(512)} %param.11) | copy-start | bytes 6148
  133.1 14.2 %collective-permute-start.1 = (bf16[512,256]{0,1:T(8,128)(2,1)S(1)}, bf16[512,256]{0,1:T(8,128)(2,1)S(1)}, u32[]{:S(2)}, u32[]{:S(2)}) collective-permute-start(bf16[512,256]{0,1:T(8,128)(2,1)S(1)} %fusion.59), channel_id=1, source_target_pairs={{2,0},{4,2},{6,4},{8,6},{10,8},{12,10},{14,12},{16,14},{18,16},{20... | collective-permute-start | bytes 786440 | tf_op jit(solution)/shard_map/ppermute | solution.py:56
  162.4 5.0 %copy-start.4 = (bf16[2048,512]{1,0:T(8,128)(2,1)S(1)}, bf16[2048,512]{1,0:T(8,128)(2,1)}, u32[]{:S(2)}) copy-start(bf16[2048,512]{1,0:T(8,128)(2,1)} %all-gather.10.cloned.1.call-done) | copy-start | bytes 6291460
  180.3 5.8 %copy-start.2 = (f32[512,4096]{1,0:T(8,128)S(1)}, f32[512,4096]{1,0:T(8,128)}, u32[]{:S(2)}) copy-start(f32[512,4096]{1,0:T(8,128)} %get-tuple-element.38) | copy-start | bytes 25165828
Sparse Core Ops, SparseCore 0:
  14.7 41.8 all-gather.7
  59.4 24.9 all-gather.13
  86.7 26.8 all-gather.15
  115.2 17.2 all-gather.9
  134.1 15.6 all-gather.11
